TPU v7x, 32 devices: a whole 2x2x4 slice. The times are simulated.
32 devices in a mesh: groups: 2 (over y), grid: 4 (over z), col: 2 (over x), sub: 2 (over core).
Axes of the slice: x: 2, y: 2, z: 4, core: 2. Of those that a mesh axis runs over, the one named last changes fastest.
Arguments:
- tokens: bfloat16 [512, 8192], P(('groups', 'grid'), ('col', 'sub')), parts along dimension 0, may hold values from -6 to 6
- teacher_gate: bfloat16 [14336, 8192], P('grid', ('col', 'sub')), may hold values from -0.0625 to 0.0625
- teacher_up: bfloat16 [14336, 8192], P('grid', ('col', 'sub')), may hold values from -0.0625 to 0.0625
- student_gate: bfloat16 [14336, 8192], P('grid', ('col', 'sub')), may hold values from -0.0625 to 0.0625
- student_up: bfloat16 [14336, 8192], P('grid', ('col', 'sub')), may hold values from -0.0625 to 0.0625
- keep_gate: int32 [112, 64], P('grid'), may hold values from -1 to 63, as said below
- keep_up: int32 [112, 64], P('grid'), may hold values from -1 to 63, as said below
Outputs:
- grad_gate: bfloat16 [28672, 8192], P(('groups', 'grid'), ('col', 'sub')), parts along dimension 0
- grad_up: bfloat16 [28672, 8192], P(('groups', 'grid'), ('col', 'sub')), parts along dimension 0
There are 2 independent parts, one for each index of `groups`. A program takes and returns all parts, laid end to end along the dimension named above; an argument that names none is the same for every part. Nothing has to cross between parts.
Inputs may be any that keep to these rules, and one draw needn't show every extreme that they name: `keep_gate`: each row lists distinct column-block numbers in rising order, then -1 to the end of the row; each row keeps at least (201) // 10 and at most 57 blocks, and some row keeps each of these two counts. `keep_up`: each row lists distinct column-block numbers in rising order, then -1 to the end of the row; each row keeps at least (201) // 10 and at most 57 blocks, and some row keeps each of these two counts.
All inputs are finite; a program needn't handle non-finite values.
Results may differ from a plain program's by a relative error of at most 0.025.
Values may be sent and summed in bfloat16 or wider, within the bound.
No kernel may reach another device: no remote copies, remote signals or barrier semaphores. Data moves between devices by JAX's collectives and lax.ppermute only.
A program may use at most 256 MiB of HBM per device.

v0:
```python
import jax
import jax.numpy as jnp
from jax import lax
from jax.sharding import PartitionSpec as P

BLOCK = 128


def local_mask(keep_rows, first_block, block_count):
    col_ids = first_block + jnp.arange(block_count, dtype=jnp.int32)
    blocks = jnp.any(keep_rows[:, :, None] == col_ids[None, None, :], axis=1)
    row_count = keep_rows.shape[0]
    tiles = jnp.broadcast_to(blocks[:, None, :, None], (row_count, BLOCK, block_count, BLOCK))
    return tiles.reshape(row_count * BLOCK, block_count * BLOCK).astype(jnp.bfloat16)


def project(rows, matrices):
    outputs = [
        lax.dot_general(rows, matrix, (((1,), (1,)), ((), ())), preferred_element_type=jnp.float32)
        for matrix in matrices
    ]
    return jnp.concatenate(outputs, axis=1)


def backprop(preacts, local_ff):
    teacher_g = preacts[:, 0:local_ff]
    teacher_u = preacts[:, local_ff : 2 * local_ff]
    student_g = preacts[:, 2 * local_ff : 3 * local_ff]
    student_u = preacts[:, 3 * local_ff : 4 * local_ff]
    sigma_s = jax.nn.sigmoid(student_g)
    sigma_t = jax.nn.sigmoid(teacher_g)
    diff = student_g * sigma_s * student_u - teacher_g * sigma_t * teacher_u
    d_gate = (diff * student_u * sigma_s * (1.0 + student_g * (1.0 - sigma_s))).astype(jnp.bfloat16)
    d_up = (diff * student_g * sigma_s).astype(jnp.bfloat16)
    return (d_gate, d_up)


def token_product(delta, tok_rows):
    return lax.dot_general(
        delta, tok_rows, (((0,), (0,)), ((), ())), preferred_element_type=jnp.float32
    )


def per_device(tokens, teacher_gate, teacher_up, student_gate, student_up, keep_gate, keep_up):
    tok_all = lax.all_gather(tokens, "grid", axis=0, tiled=True)
    local_ff = student_gate.shape[0]
    local_d = student_gate.shape[1]
    block_count = local_d // BLOCK
    first_block = lax.axis_index(("col", "sub")) * block_count
    mask_gate = local_mask(keep_gate, first_block, block_count)
    mask_up = local_mask(keep_up, first_block, block_count)
    matrices = (teacher_gate, teacher_up, student_gate * mask_gate, student_up * mask_up)
    rows = tok_all
    preacts = lax.psum_scatter(
        project(rows, matrices).astype(jnp.bfloat16),
        ("col", "sub"),
        scatter_dimension=0,
        tiled=True,
    ).astype(jnp.float32)
    d_gate, d_up = backprop(preacts, local_ff)
    rows = tok_all
    sum_gate = token_product(lax.all_gather(d_gate, ("col", "sub"), axis=0, tiled=True), rows)
    sum_up = token_product(lax.all_gather(d_up, ("col", "sub"), axis=0, tiled=True), rows)
    grad_gate = (sum_gate * mask_gate).astype(jnp.bfloat16)
    grad_up = (sum_up * mask_up).astype(jnp.bfloat16)
    return (grad_gate, grad_up)


def solution(mesh):
    return jax.shard_map(
        per_device,
        mesh=mesh,
        in_specs=(
            P(("groups", "grid"), ("col", "sub")),
            P("grid", ("col", "sub")),
            P("grid", ("col", "sub")),
            P("grid", ("col", "sub")),
            P("grid", ("col", "sub")),
            P("grid", None),
            P("grid", None),
        ),
        out_specs=(P(("groups", "grid"), ("col", "sub")), P(("groups", "grid"), ("col", "sub"))),
        check_vma=False,
    )
```

profile of v0, /device:TPU:19, one launch (start us, length us, event | category | flops | bytes accessed | tf_op | source)
XLA Modules:
  0.0 218.4 jit_solution(7881793862161127962)
XLA Ops:
  7.2 0.0 all-gather.4.cloned.1.call-start
  7.2 0.7 all-gather.4.cloned.1.call-update
  7.9 0.0 reduce-scatter.2.cloned.1.call-start
  8.0 1.8 compare_reduce_fusion.1
  9.8 28.3 %all-gather.4.cloned.1.call-done = bf16[256,2048]{1,0:T(8,128)(2,1)} async-done(((bf16[64,2048]{1,0:T(8,128)(2,1)}), bf16[256,2048]{1,0:T(8,128)(2,1)}) %all-gather.4.cloned.1.call-update) | async-done | bytes 1048592 | tf_op jit(solution)/shard_map/all_gather | solution.py:45
  38.1 9.6 %convolution_convert_fusion = bf16[256,3584]{1,0:T(8,128)(2,1)S(1)} fusion(bf16[256,2048]{1,0:T(8,128)(2,1)} %all-gather.4.cloned.1.call-done, bf16[3584,2048]{1,0:T(8,128)(2,1)} %param.9), kind=kOutput, calls=%fused_computation.13 | convolution fusion | flops 3759013888 | bytes 17563648 | tf_op jit(solution)/shard_map/dot_general | solution.py:19
  47.7 9.2 %convolution_convert_fusion.1 = bf16[256,3584]{1,0:T(8,128)(2,1)S(1)} fusion(bf16[256,2048]{1,0:T(8,128)(2,1)S(1)} %copy-done.3, bf16[3584,2048]{1,0:T(8,128)(2,1)} %param.8), kind=kOutput, calls=%fused_computation.14 | convolution fusion | flops 3759013888 | bytes 17563648 | tf_op jit(solution)/shard_map/dot_general | solution.py:19
  56.8 2.0 broadcast_in_dim.4
  58.8 12.3 %fusion.6 = bf16[256,3584]{1,0:T(8,128)(2,1)} fusion(bf16[256,2048]{1,0:T(8,128)(2,1)S(1)} %copy-done.3, bf16[3584,2048]{1,0:T(8,128)(2,1)} %param.10, pred[448,8,16,128]{3,2,1,0:T(8,128)(4,1)S(1)} %bitcast.40), kind=kOutput, calls=%fused_computation.15 | convolution fusion | flops 3766353920 | bytes 24903680 | tf_op jit(solution)/shard_map/dot_general | solution.py:19
  71.1 2.0 broadcast_in_dim.5
  73.1 11.5 %fusion.7 = bf16[256,3584]{1,0:T(8,128)(2,1)S(1)} fusion(bf16[256,2048]{1,0:T(8,128)(2,1)S(1)} %copy-done.3, bf16[3584,2048]{1,0:T(8,128)(2,1)} %param.11, pred[448,8,16,128]{3,2,1,0:T(8,128)(4,1)S(1)} %bitcast.38), kind=kOutput, calls=%fused_computation.16 | convolution fusion | flops 3766353920 | bytes 24903680 | tf_op jit(solution)/shard_map/dot_general | solution.py:19
  84.6 3.3 %pad_maximum_fusion = bf16[256,14336]{1,0:T(8,128)(2,1)} fusion(bf16[256,3584]{1,0:T(8,128)(2,1)S(1)} %fusion.7, bf16[256,3584]{1,0:T(8,128)(2,1)S(1)} %copy-done.2, bf16[256,3584]{1,0:T(8,128)(2,1)S(1)} %convolution_convert_fusion, bf16[256,3584]{1,0:T(8,128)(2,1)S(1)} %convolution_convert_fusion.1), kind=kLoop, calls=%fused_computation.8 | loop fusion | flops 29360128 | bytes 14680064 | tf_op jit(solution)/shard_map/concatenate | solution.py:22
  87.9 0.0 all-gather.6.cloned.1.call-start
  88.0 64.6 %reduce-scatter.2.cloned.1.call-done = bf16[64,14336]{1,0:T(8,128)(2,1)} async-done(((bf16[256,14336]{1,0:T(8,128)(2,1)}), bf16[64,14336]{1,0:T(8,128)(2,1)}) %reduce-scatter.2.cloned.1.call-update) | async-done | bytes 1835024 | tf_op jit(solution)/shard_map/reduce_scatter | solution.py:54
  152.6 1.7 convert_element_type.28
  154.3 1.3 multiply_convert_fusion.2
  155.6 1.1 multiply_convert_fusion.3
  156.7 0.0 all-gather.6.cloned.1.call-update
  156.8 0.0 all-gather.8.cloned.1.call-start
  156.8 0.5 all-gather.8.cloned.1.call-update
  157.3 21.1 %all-gather.6.cloned.1.call-done = bf16[256,3584]{1,0:T(8,128)(2,1)} async-done(((bf16[64,3584]{1,0:T(8,128)(2,1)}), bf16[256,3584]{1,0:T(8,128)(2,1)}) %all-gather.6.cloned.1.call-update) | async-done | bytes 1835024 | tf_op jit(solution)/shard_map/all_gather | solution.py:62
  178.4 10.2 %multiply_convert_fusion.1 = bf16[3584,2048]{1,0:T(8,128)(2,1)} fusion(bf16[256,3584]{1,0:T(8,128)(2,1)} %all-gather.6.cloned.1.call-done, bf16[256,2048]{1,0:T(8,128)(2,1)S(1)} %copy-done.3, pred[448,8,16,128]{3,2,1,0:T(8,128)(4,1)} %bitcast.41), kind=kOutput, calls=%fused_computation.1 | convolution fusion | flops 3787456512 | bytes 24903680 | tf_op jit(solution)/shard_map/dot_general | solution.py:39
  188.6 13.0 %all-gather.8.cloned.1.call-done = bf16[256,3584]{1,0:T(8,128)(2,1)} async-done(((bf16[64,3584]{1,0:T(8,128)(2,1)}), bf16[256,3584]{1,0:T(8,128)(2,1)}) %all-gather.8.cloned.1.call-update) | async-done | bytes 1835024 | tf_op jit(solution)/shard_map/all_gather | solution.py:63
  201.7 10.2 %multiply_convert_fusion = bf16[3584,2048]{1,0:T(8,128)(2,1)} fusion(bf16[256,3584]{1,0:T(8,128)(2,1)} %all-gather.8.cloned.1.call-done, bf16[256,2048]{1,0:T(8,128)(2,1)S(1)} %copy-done.3, pred[448,8,16,128]{3,2,1,0:T(8,128)(4,1)} %bitcast.39), kind=kOutput, calls=%fused_computation | convolution fusion | flops 3787456512 | bytes 24903680 | tf_op jit(solution)/shard_map/dot_general | solution.py:39
  (10 shorter events, 0.0 us)
Async XLA Ops:
  7.2 30.9 %all-gather.4.cloned.1.call-start = ((), (), s32[]{:S(2)}) async-start(), calls=%async_computation.1 | async-start | bytes 1310720 | tf_op jit(solution)/shard_map/all_gather | solution.py:45
  7.9 144.7 %reduce-scatter.2.cloned.1.call-start = ((), (), s32[]{:S(2)}) async-start(), calls=%async_computation.2 | async-start | bytes 9175040 | tf_op jit(solution)/shard_map/reduce_scatter | solution.py:54
  38.1 9.6 %copy-start.3 = (bf16[256,2048]{1,0:T(8,128)(2,1)S(1)}, bf16[256,2048]{1,0:T(8,128)(2,1)}, u32[]{:S(2)}) copy-start(bf16[256,2048]{1,0:T(8,128)(2,1)} %all-gather.4.cloned.1.call-done) | copy-start | bytes 3145732
  58.8 12.3 %copy-start.1 = (pred[28,128,16,128]{3,2,1,0:T(8,128)(4,1)}, pred[28,128,16,128]{3,2,1,0:T(8,128)(4,1)S(1)}, u32[]{:S(2)}) copy-start(pred[28,128,16,128]{3,2,1,0:T(8,128)(4,1)S(1)} %broadcast_in_dim.4) | copy-start | bytes 22020100
  73.1 11.5 %copy-start = (pred[28,128,16,128]{3,2,1,0:T(8,128)(4,1)}, pred[28,128,16,128]{3,2,1,0:T(8,128)(4,1)S(1)}, u32[]{:S(2)}) copy-start(pred[28,128,16,128]{3,2,1,0:T(8,128)(4,1)S(1)} %broadcast_in_dim.5) | copy-start | bytes 22020100
  73.1 11.5 %copy-start.2 = (bf16[256,3584]{1,0:T(8,128)(2,1)S(1)}, bf16[256,3584]{1,0:T(8,128)(2,1)}, u32[]{:S(2)}) copy-start(bf16[256,3584]{1,0:T(8,128)(2,1)} %fusion.6) | copy-start | bytes 5505028
  87.9 90.5 %all-gather.6.cloned.1.call-start = ((), (), s32[]{:S(2)}) async-start(), calls=%async_computation.3 | async-start | bytes 2293760 | tf_op jit(solution)/shard_map/all_gather | solution.py:62
  156.8 44.9 %all-gather.8.cloned.1.call-start = ((), (), s32[]{:S(2)}) async-start(), calls=%async_computation.4 | async-start | bytes 2293760 | tf_op jit(solution)/shard_map/all_gather | solution.py:63
Sparse Core Ops, SparseCore 0:
  9.6 28.4 all-gather.3
  88.0 64.4 reduce-scatter.1
  156.9 21.5 all-gather.5
  180.5 21.1 all-gather.7
where the time goes:
time: 221 us; the launch traced here: 218 us
  waiting for transfers between devices  128 us (58%)
  matrix products  62.9 us (28%)
  between operations  13.9 us (6%)
  other arithmetic  9.3 us (4%)
  local copies, waits for them, and re-layouts  3.93 us (2%)
    reduce_scatter x1, waiting for transfers between devices, per_device(): lax.psum_scatter(project(rows, matrices).astype(jnp.bfloat16), ('col', 's...  64.6 us
    dot_general x4, matrix products, project(): lax.dot_general(rows, matrix, (((1,), (1,)), ((), ())), preferred_element...  42.5 us
    all_gather x1, waiting for transfers between devices, per_device(): tok_all = lax.all_gather(tokens, 'grid', axis=0, tiled=True)  28.3 us
    all_gather x1, waiting for transfers between devices, per_device(): lax.all_gather(d_gate, ('col', 'sub'), axis=0, tiled=True)  21.1 us
    dot_general x2, matrix products, token_product(): lax.dot_general(delta, tok_rows, (((0,), (0,)), ((), ())), preferred_elem...  20.4 us
    all_gather x1, waiting for transfers between devices, per_device(): lax.all_gather(d_up, ('col', 'sub'), axis=0, tiled=True)  13 us
  transfers between devices with their start and end apart: 4, of which 4 were waited for; matrix products, arithmetic and copies ran while one was open for 6% of the time, Pallas kernels for 0%

commit v1 on v0

v1 whole, which is shorter than its diff:
```python
import functools
import math

import jax
import jax.numpy as jnp
from jax import lax
from jax.experimental import pallas as pl
from jax.experimental.pallas import tpu as pltpu
from jax.sharding import PartitionSpec as P

BLOCK = 128
SLOTS = 6
OUT_SLOTS = 4
PARTS = (2, 3, 2)
ORDER = ("F0", "S0", "F1+", "D0+", "S1", "F2+", "R0", "D1", "G0+", "S2", "R1", "G1", "D2", "R2", "G2")
HBM = pl.BlockSpec(memory_space=pltpu.HBM)
ANY = pl.BlockSpec(memory_space=pl.ANY)
VM = pl.BlockSpec(memory_space=pltpu.VMEM)
SM = pl.BlockSpec(memory_space=pltpu.SMEM)
LONG = pl.CostEstimate(flops=2 * 10**10, bytes_accessed=1, transcendentals=0)
SHORT = pl.CostEstimate(flops=1, bytes_accessed=1, transcendentals=0)


def params(mib):
    return pltpu.CompilerParams(vmem_limit_bytes=mib * 2**20)


def mask_rows(keep_rows, first_block, block_count, group):
    col_ids = first_block + jnp.arange(block_count, dtype=jnp.int32)
    blocks = jnp.any(keep_rows[:, :, None] == col_ids[None, None, :], axis=1).astype(jnp.float32)
    blocks = jnp.repeat(blocks, BLOCK // group, axis=0)
    return jnp.repeat(blocks, BLOCK, axis=1)[:, None, :]


def forward_kernel(g, first, nx, nq, where, tok, mg, mu, w0, w1, w2, w3, *rest):
    sib, own, buf, held, sem, out_sem = rest[-6:]
    weights, masks = (w0, w1, w2, w3), (mg, mu)
    depth = tok.shape[1]
    steps = 2 * nx * nq

    def offset_of(part):
        return lax.rem(lax.rem(part, nx) + 1, nx)

    def group_of(i):
        part = i // nq
        side = lax.rem(where[0] + 1 + part // nx, 2)
        piece = lax.rem(where[1] + offset_of(part), nx)
        return first + (side * nx + piece) * nq + lax.rem(i, nq)

    def copies(i):
        slot = lax.rem(i, SLOTS)
        start = pl.multiple_of(group_of(i) * g, g)
        return [
            pltpu.make_async_copy(weights[m].at[pl.ds(start, g)], buf.at[slot, m], sem.at[slot, m]) for m in range(4)
        ]

    def start_all(i):
        for copy in copies(i):
            copy.start()

    pl.loop(0, min(SLOTS - 1, steps))(start_all)

    @pl.loop(0, steps)
    def _(i):
        slot = lax.rem(i, SLOTS)
        for copy in copies(i):
            copy.wait()
        pl.when(i + SLOTS - 1 < steps)(lambda: start_all(i + SLOTS - 1))
        for m in (2, 3):
            buf[slot, m] = buf[slot, m] * masks[m - 2][group_of(i)].astype(jnp.bfloat16)
        sums = lax.dot_general(
            buf[slot].reshape(4 * g, depth), tok[...], (((1,), (1,)), ((), ())), preferred_element_type=jnp.float32
        ).astype(jnp.bfloat16)
        part = i // nq
        rows = pl.ds(pl.multiple_of(lax.rem(i, nq) * g, g), g)
        for m in range(4):
            held[part, m, rows] = sums[m * g : (m + 1) * g]

        @pl.when(lax.rem(i, nq) == nq - 1)
        def _():
            @pl.when(part < nx)
            def _():
                pltpu.make_async_copy(held.at[part], sib.at[offset_of(part)], out_sem.at[part]).start()

            @pl.when(part >= nx)
            def _():
                pltpu.make_async_copy(held.at[part], own.at[offset_of(part)], out_sem.at[part]).start()

    for part in range(2 * nx):
        target = sib if part < nx else own
        pltpu.make_async_copy(held.at[part], target.at[(part % nx + 1) % nx], out_sem.at[part]).wait()


def forward_call(g, first, nx, nq, where, tok, masks, weights, after, cost):
    count, depth = tok.shape
    rows = 2 * nx * nq * g
    shape = jax.ShapeDtypeStruct((nx, 4, nq * g, count), jnp.bfloat16)
    return pl.pallas_call(
        functools.partial(forward_kernel, g, first, nx, nq),
        in_specs=[SM, VM, VM, VM] + [HBM] * 4 + [ANY] * len(after),
        out_specs=(ANY, ANY),
        out_shape=(shape, shape),
        scratch_shapes=[
            pltpu.VMEM((SLOTS, 4, g, depth), jnp.bfloat16),
            pltpu.VMEM((2 * nx, 4, nq * g, count), jnp.bfloat16),
            pltpu.SemaphoreType.DMA((SLOTS, 4)),
            pltpu.SemaphoreType.DMA((2 * nx,)),
        ],
        compiler_params=params(44),
        cost_estimate=cost,
        name="forward",
    )(where, tok, *masks, *weights, *after)


def sum_kernel(count, *refs):
    own, got = refs[0], refs[1]
    outs = refs[-count:]
    for k, out in enumerate(outs):
        out[...] = (own[k + 1].astype(jnp.float32) + got[k + 1].astype(jnp.float32)).astype(jnp.bfloat16)


def sum_call(nx, own, got, after):
    shape = own.shape[1:]
    step = min(64, shape[1])
    block = pl.BlockSpec((nx,) + (4, step, shape[2]), lambda i: (0, 0, i, 0))
    out_block = pl.BlockSpec((4, step, shape[2]), lambda i: (0, i, 0))
    size = math.prod(shape)
    return pl.pallas_call(
        functools.partial(sum_kernel, nx - 1),
        grid=(shape[1] // step,),
        in_specs=[block, block] + [ANY] * len(after),
        out_specs=[out_block] * (nx - 1),
        out_shape=[jax.ShapeDtypeStruct(shape, jnp.bfloat16)] * (nx - 1),
        compiler_params=params(16),
        cost_estimate=SHORT,
        name="sums",
    )(own, got, *after)


def delta_kernel(count, own, got, *refs):
    arrived, out = refs[:count], refs[-1]

    def total(m):
        value = own[0, m].astype(jnp.float32) + got[0, m].astype(jnp.float32)
        for ref in arrived:
            value = value + ref[m].astype(jnp.float32)
        return value

    teacher_g, teacher_u, student_g, student_u = total(0), total(1), total(2), total(3)
    sigma_s = jax.nn.sigmoid(student_g)
    sigma_t = jax.nn.sigmoid(teacher_g)
    diff = student_g * sigma_s * student_u - teacher_g * sigma_t * teacher_u
    out[0] = (diff * student_u * sigma_s * (1.0 + student_g * (1.0 - sigma_s))).astype(jnp.bfloat16)
    out[1] = (diff * student_g * sigma_s).astype(jnp.bfloat16)


def delta_call(nx, own, got, arrived, after, cost):
    rows, count = own.shape[2:]
    step = min(64, rows)
    first = pl.BlockSpec((1, 4, step, count), lambda i: (0, 0, i, 0))
    other = pl.BlockSpec((4, step, count), lambda i: (0, i, 0))
    return pl.pallas_call(
        functools.partial(delta_kernel, nx - 1),
        grid=(rows // step,),
        in_specs=[first, first] + [other] * (nx - 1) + [ANY] * len(after),
        out_specs=pl.BlockSpec((2, step, count), lambda i: (0, i, 0)),
        out_shape=jax.ShapeDtypeStruct((2, rows, count), jnp.bfloat16),
        compiler_params=params(16),
        cost_estimate=cost,
        name="deltas",
    )(own, got, *arrived, *after)


def relay_kernel(count, *refs):
    for source, target in zip(refs[:count], refs[-count:]):
        target[...] = source[...]


def relay_call(pieces, after):
    count = len(pieces)
    return pl.pallas_call(
        functools.partial(relay_kernel, count),
        in_specs=[VM] * count + [ANY] * len(after),
        out_specs=[VM] * count,
        out_shape=[jax.ShapeDtypeStruct(x.shape, x.dtype) for x in pieces],
        compiler_params=params(16),
        cost_estimate=SHORT,
        name="relay",
    )(*pieces, *after)


def grads_kernel(g, first, nx, nq, count, width, where, tok, mg, mu, *refs):
    deltas = refs[:count]
    gate, up, _, left, buf, in_sem, out_sem = refs[-7:]
    masks, outs = (mg, mu), (gate, up)
    rows = nq * g
    steps = 2 * (tok.shape[1] // width)
    arrivals = [pltpu.make_async_copy(deltas[b], left.at[:, b], in_sem.at[b]) for b in range(count)]
    for copy in arrivals:
        copy.start()

    groups = []
    for b in range(count):
        side = lax.rem(where[0] + b // nx, 2)
        groups.append(first + (side * nx + lax.rem(where[1] + nx - b % nx, nx)) * nq)

    def columns(t):
        return pl.ds(pl.multiple_of((t // 2) * width, width), width)

    def leave(t, m):
        slot = lax.rem(t, OUT_SLOTS)
        return [
            pltpu.make_async_copy(
                buf.at[slot, b],
                outs[m].at[pl.ds(pl.multiple_of(groups[b] * g, g), rows), columns(t)],
                out_sem.at[slot, b],
            )
            for b in range(count)
        ]

    for copy in arrivals:
        copy.wait()

    @pl.loop(0, steps)
    def _(t):
        slot, m, cols = lax.rem(t, OUT_SLOTS), lax.rem(t, 2), columns(t)

        @pl.when(t >= OUT_SLOTS)
        def _():
            for copy in leave(t - OUT_SLOTS, 0):
                copy.wait()

        sums = jnp.dot(
            left[m].reshape(count * rows, left.shape[3]), tok[:, cols], preferred_element_type=jnp.float32
        ).astype(jnp.bfloat16)
        for b in range(count):
            for r in range(nq):
                gate_row = masks[0][groups[b] + r, :, cols]
                up_row = masks[1][groups[b] + r, :, cols]
                row = jnp.where(m == 0, gate_row, up_row).astype(jnp.bfloat16)
                at = b * rows + r * g
                buf[slot, b, r * g : (r + 1) * g] = sums[at : at + g] * row
        for which in range(2):

            @pl.when(m == which)
            def _():
                for copy in leave(t, which):
                    copy.start()

    for t in range(max(0, steps - OUT_SLOTS), steps):
        for copy in leave(t, t % 2):
            copy.wait()


def grads_call(g, first, nx, nq, where, tok, masks, deltas, grads, shape, after, cost):
    tokens, depth = tok.shape
    rows = nq * g
    count = len(deltas)
    width = min(512, depth)
    held = [] if grads is None else list(grads)
    base = 4 + count
    grad = jax.ShapeDtypeStruct(shape, jnp.bfloat16)
    return pl.pallas_call(
        functools.partial(grads_kernel, g, first, nx, nq, count, width),
        in_specs=[SM, VM, VM, VM] + [ANY] * count + [HBM] * len(held) + [ANY] * len(after),
        out_specs=(HBM, HBM, ANY),
        out_shape=(grad, grad, jax.ShapeDtypeStruct((8, BLOCK), jnp.float32)),
        scratch_shapes=[
            pltpu.VMEM((2, count, rows, tokens), jnp.bfloat16),
            pltpu.VMEM((OUT_SLOTS, count, rows, width), jnp.bfloat16),
            pltpu.SemaphoreType.DMA((count,)),
            pltpu.SemaphoreType.DMA((OUT_SLOTS, count)),
        ],
        input_output_aliases={base: 0, base + 1: 1} if held else {},
        compiler_params=params(44),
        cost_estimate=cost,
        name="grads",
    )(where, tok, *masks, *deltas, *held, *after)


def per_device(nx, nz, tokens, teacher_gate, teacher_up, student_gate, student_up, keep_gate, keep_up):
    local_ff, local_d = student_gate.shape
    g = math.gcd(local_ff // (2 * nx), BLOCK)
    block_count = local_d // BLOCK
    first_block = lax.axis_index(("col", "sub")) * block_count
    masks = [mask_rows(keep, first_block, block_count, g) for keep in (keep_gate, keep_up)]
    weights = (teacher_gate, teacher_up, student_gate, student_up)
    where = jnp.stack([lax.axis_index("sub"), lax.axis_index("col")]).astype(jnp.int32)

    def swap(x):
        return lax.ppermute(x, "sub", [(0, 1), (1, 0)])

    def turn(x, k):
        return lax.ppermute(x, "col", [(i, (i + k) % nx) for i in range(nx)])

    if nz == 4:
        others = [lax.ppermute(tokens, "grid", [(i, i ^ k) for i in range(nz)]) for k in (1, 2, 3)]
        tok = jnp.concatenate([tokens] + others, axis=0)
    else:
        tok = lax.all_gather(tokens, "grid", axis=0, tiled=True)

    total = local_ff // (2 * nx * g)
    if sum(PARTS) == total:
        parts, order = PARTS, ORDER
    else:
        parts = (1,) * total
        order = [kind + str(u) for u in range(total) for kind in "FSDRG"]
    grads = None
    units = [(sum(parts[:u]) * 2 * nx, nq) for u, nq in enumerate(parts)]
    state = {}
    after = ()
    for step in order:
        kind, u = step[0], int(step[1])
        cost = LONG if step.endswith("+") else SHORT
        first, nq = units[u]
        if kind == "F":
            sib, own = forward_call(g, first, nx, nq, where, tok, masks, weights, after, cost)
            state[u] = (own, swap(sib))
            after = (own,)
        elif kind == "S":
            own, got = state[u]
            sends = sum_call(nx, own, got, after)
            state[u] = (own, got, [turn(sends[k - 1], k) for k in range(1, nx)])
            after = (sends[0],)
        elif kind == "D":
            own, got, arrived = state[u]
            mine = delta_call(nx, own, got, arrived, after, cost)
            state[u] = ([mine, swap(mine)], [turn(mine, k) for k in range(1, nx)])
            after = (mine,)
        elif kind == "R":
            (mine, theirs), far = state[u]
            near = relay_call(far, after)
            state[u] = [mine, *near, theirs, *[swap(x) for x in near]]
            after = (near[0],)
        else:
            *grads, done = grads_call(
                g, first, nx, nq, where, tok, masks, state[u], grads, (local_ff, local_d), after, cost
            )
            after = (done,)
    return tuple(grads)


def solution(mesh):
    return jax.shard_map(
        functools.partial(per_device, mesh.shape["col"], mesh.shape["grid"]),
        mesh=mesh,
        in_specs=(
            P(("groups", "grid"), ("col", "sub")),
            P("grid", ("col", "sub")),
            P("grid", ("col", "sub")),
            P("grid", ("col", "sub")),
            P("grid", ("col", "sub")),
            P("grid", None),
            P("grid", None),
        ),
        out_specs=(P(("groups", "grid"), ("col", "sub")), P(("groups", "grid"), ("col", "sub"))),
        check_vma=False,
    )
```

time: 221 us -> 118 us (0.53)
  waiting for transfers between devices: 128 us -> 44 us
  matrix products: 62.9 us -> 0 us
  Pallas kernels: 0 us -> 50.8 us
  starting transfers between devices: 0.16 us -> 18.5 us
  between operations: 13.9 us -> 0.84 us
  other arithmetic: 9.3 us -> 1.92 us
  local copies, waits for them, and re-layouts: 3.93 us -> 1.29 us
    reduce_scatter x1 -> x0, waiting for transfers between devices: 64.6 us -> none  [per_device(): lax.psum_scatter(project(rows, matrices).astype(jnp.bfloat16), ('col', 's...]
    dot_general x6 -> x0, matrix products: 62.9 us -> none  [the longest x4 42.5 us: project(): lax.dot_general(rows, matrix, (((1,), (1,)), ((), ())), preferred_element...]
    all_gather x3 -> x0, waiting for transfers between devices: 62.4 us -> none  [the longest x1 28.3 us: per_device(): tok_all = lax.all_gather(tokens, 'grid', axis=0, tiled=True)]
    pallas_call x0 -> x15, Pallas kernels: none -> 50.8 us  [the longest x3 29.5 us: forward_call(): pl.pallas_call(functools.partial(forward_kernel, g, first, nx, nq), in_sp...]
    ppermute x0 -> x18, waiting for transfers between devices: none -> 44 us  [the longest x3 20.5 us: per_device(): lax.ppermute(tokens, 'grid', [(i, i ^ k) for i in range(nz)])]
    ppermute x0 -> x18, starting transfers between devices: none -> 18.5 us  [the longest x9 12.1 us: swap(): return lax.ppermute(x, 'sub', [(0, 1), (1, 0)])]
    convert_element_type x3 -> x2, other arithmetic: 4.15 us -> 0.01 us  [mask_rows(): jnp.any(keep_rows[:, :, None] == col_ids[None, None, :], axis=1)]
    broadcast_in_dim x2, local copies, waits for them, and re-layouts: 3.91 us -> 0.23 us  [mask_rows(): return jnp.repeat(blocks, BLOCK, axis=1)[:, None, :]]
  transfers between devices with their start and end apart: 4 -> 18, of which waited for: 4 -> 10; matrix products, arithmetic and copies ran while one was open for 6% -> 3% of each run, Pallas kernels for 0% -> 30%
where the time goes in v1:
time: 118 us; the launch traced here: 117 us
  Pallas kernels  50.8 us (43%)
  waiting for transfers between devices  44 us (37%)
  starting transfers between devices  18.5 us (16%)
  other arithmetic  1.92 us (2%)
  local copies, waits for them, and re-layouts  1.29 us (1%)
    pallas_call x3, Pallas kernels, forward_call(): pl.pallas_call(functools.partial(forward_kernel, g, first, nx, nq), in_sp...  29.5 us
    ppermute x3, waiting for transfers between devices, per_device(): lax.ppermute(tokens, 'grid', [(i, i ^ k) for i in range(nz)])  20.5 us
    ppermute x6, waiting for transfers between devices, turn(): return lax.ppermute(x, 'col', [(i, (i + k) % nx) for i in range(nx)])  17.9 us
    pallas_call x3, Pallas kernels, grads_call(): pl.pallas_call(functools.partial(grads_kernel, g, first, nx, nq, count, w...  17.9 us
    ppermute x9, starting transfers between devices, swap(): return lax.ppermute(x, 'sub', [(0, 1), (1, 0)])  12.1 us
    ppermute x9, waiting for transfers between devices, swap(): return lax.ppermute(x, 'sub', [(0, 1), (1, 0)])  5.53 us
    ppermute x6, starting transfers between devices, turn(): return lax.ppermute(x, 'col', [(i, (i + k) % nx) for i in range(nx)])  3.68 us
    ppermute x3, starting transfers between devices, per_device(): lax.ppermute(tokens, 'grid', [(i, i ^ k) for i in range(nz)])  2.71 us
  transfers between devices with their start and end apart: 18, of which 10 were waited for; matrix products, arithmetic and copies ran while one was open for 3% of the time, Pallas kernels for 30%

profile of v1, /device:TPU:19, one launch (start us, length us, event | category | flops | bytes accessed | tf_op | source)
XLA Modules:
  0.0 117.3 jit_solution(10257137166282879136)
XLA Ops:
  0.8 1.3 %collective-permute-start = (bf16[64,2048]{1,0:T(8,128)(2,1)}, bf16[64,2048]{1,0:T(8,128)(2,1)S(1)}, u32[]{:S(2)}, u32[]{:S(2)}) collective-permute-start(bf16[64,2048]{1,0:T(8,128)(2,1)} %param.7), channel_id=1, source_target_pairs={{0,4},{4,0},{8,12},{12,8},{1,5},{5,1},{9,13},{13,9},{2,6},{6,2},{1... | collective-permute-start | bytes 786440 | tf_op jit(solution)/shard_map/ppermute | solution.py:297
  2.1 1.3 %collective-permute-start.2 = (bf16[64,2048]{1,0:T(8,128)(2,1)}, bf16[64,2048]{1,0:T(8,128)(2,1)S(1)}, u32[]{:S(2)}, u32[]{:S(2)}) collective-permute-start(bf16[64,2048]{1,0:T(8,128)(2,1)} %param.7), channel_id=1, source_target_pairs={{0,12},{4,8},{8,4},{12,0},{1,13},{5,9},{9,5},{13,1},{2,14},{6,10},... | collective-permute-start | bytes 786440 | tf_op jit(solution)/shard_map/ppermute | solution.py:297
  3.3 1.0 constant_dynamic-update-slice_fusion.3
  4.4 1.8 %compare_reduce_fusion = (pred[28,16]{1,0:T(8,128)(4,1)S(1)}, pred[28,16]{1,0:T(8,128)(4,1)S(1)}) fusion(s32[28,64]{1,0:T(8,128)} %param.13, s32[16]{0:T(128)S(1)} %iota_add_fusion, s32[28,64]{1,0:T(8,128)} %param.12), kind=kLoop, calls=%fused_computation | loop fusion | flops 113792 | bytes 15296 | tf_op jit(solution)/shard_map/reduce_or | solution.py:30
  6.3 7.4 %collective-permute-done = bf16[64,2048]{1,0:T(8,128)(2,1)S(1)} collective-permute-done((bf16[64,2048]{1,0:T(8,128)(2,1)}, bf16[64,2048]{1,0:T(8,128)(2,1)S(1)}, u32[]{:S(2)}, u32[]{:S(2)}) %collective-permute-start) | collective-permute-done | bytes 262176 | tf_op jit(solution)/shard_map/ppermute | solution.py:297
  13.7 13.2 %collective-permute-done.2 = bf16[64,2048]{1,0:T(8,128)(2,1)S(1)} collective-permute-done((bf16[64,2048]{1,0:T(8,128)(2,1)}, bf16[64,2048]{1,0:T(8,128)(2,1)S(1)}, u32[]{:S(2)}, u32[]{:S(2)}) %collective-permute-start.2) | collective-permute-done | bytes 262176 | tf_op jit(solution)/shard_map/ppermute | solution.py:297
  27.2 8.8 %forward.3 = (bf16[2,4,256,256]{3,2,1,0:T(8,128)(2,1)S(1)}, bf16[2,4,256,256]{3,2,1,0:T(8,128)(2,1)S(1)}) custom-call(s32[2]{0:T(128)S(1)} %pad_add_fusion.where, bf16[256,2048]{1,0:T(8,128)(2,1)S(1)} %constant_dynamic-update-slice_fusion.tok, f32[28,1,2048]{2,1,0:T(1,128)S(1)} %bitcast.4, f32[28,1,2048]{2,1,0:T(1,128)S(1)} %bitcast.10, ...), custom_call_target="tpu_custom_call" | custom-call | flops 1 | bytes 1 | tf_op jit(solution)/shard_map/forward/pallas_call | solution.py:98
  36.5 2.3 %collective-permute-done.3.refs_1_.got = bf16[2,4,256,256]{3,2,1,0:T(8,128)(2,1)S(1)} collective-permute-done((bf16[2,4,256,256]{3,2,1,0:T(8,128)(2,1)S(1)}, bf16[2,4,256,256]{3,2,1,0:T(8,128)(2,1)S(1)}, u32[]{:S(2)}, u32[]{:S(2)}) %collective-permute-start.3) | collective-permute-done | bytes 1048608 | tf_op jit(solution)/shard_map/ppermute | solution.py:291
  39.5 12.0 %forward.4 = (bf16[2,4,384,256]{3,2,1,0:T(8,128)(2,1)S(1)}, bf16[2,4,384,256]{3,2,1,0:T(8,128)(2,1)S(1)}) custom-call(s32[2]{0:T(128)S(1)} %pad_add_fusion.where, bf16[256,2048]{1,0:T(8,128)(2,1)S(1)} %constant_dynamic-update-slice_fusion.tok, f32[28,1,2048]{2,1,0:T(1,128)S(1)} %bitcast.5, f32[28,1,2048]{2,1,0:T(1,128)S(1)} %bitcast.11, ...), custom_call_target="tpu_custom_call" | custom-call | flops 20000000000 | bytes 1 | tf_op jit(solution)/shard_map/forward/pallas_call | solution.py:98
  52.9 1.3 %collective-permute-start.8 = (bf16[2,256,256]{2,1,0:T(8,128)(2,1)S(1)}, bf16[2,256,256]{2,1,0:T(8,128)(2,1)S(1)}, u32[]{:S(2)}, u32[]{:S(2)}) collective-permute-start(bf16[2,256,256]{2,1,0:T(8,128)(2,1)S(1)} %deltas.3.refs_2_.refs_0_), channel_id=1, source_target_pairs={{0,1},{1,0},{2,3},{3,2},{4,5},{5,4},{6,7},{7,6},{8,9},{9,8},{10,11... | collective-permute-start | bytes 786440 | tf_op jit(solution)/shard_map/ppermute | solution.py:291
  55.8 1.3 %collective-permute-start.10 = (bf16[4,384,256]{2,1,0:T(8,128)(2,1)S(1)}, bf16[4,384,256]{2,1,0:T(8,128)(2,1)S(1)}, u32[]{:S(2)}, u32[]{:S(2)}) collective-permute-start(bf16[4,384,256]{2,1,0:T(8,128)(2,1)S(1)} %sums.4.rest_0_), channel_id=1, source_target_pairs={{0,2},{2,0},{1,3},{3,1},{4,6},{6,4},{5,7},{7,5},{8,10},{10,8},{9,1... | collective-permute-start | bytes 2359304 | tf_op jit(solution)/shard_map/ppermute | solution.py:294
  57.1 8.8 %forward.5 = (bf16[2,4,256,256]{3,2,1,0:T(8,128)(2,1)S(1)}, bf16[2,4,256,256]{3,2,1,0:T(8,128)(2,1)S(1)}) custom-call(s32[2]{0:T(128)S(1)} %pad_add_fusion.where, bf16[256,2048]{1,0:T(8,128)(2,1)S(1)} %constant_dynamic-update-slice_fusion.tok, f32[28,1,2048]{2,1,0:T(1,128)S(1)} %bitcast.6, f32[28,1,2048]{2,1,0:T(1,128)S(1)} %bitcast.12, ...), custom_call_target="tpu_custom_call" | custom-call | flops 20000000000 | bytes 1 | tf_op jit(solution)/shard_map/forward/pallas_call | solution.py:98
  66.7 12.3 %collective-permute-done.10.refs_0_ = bf16[4,384,256]{2,1,0:T(8,128)(2,1)S(1)} collective-permute-done((bf16[4,384,256]{2,1,0:T(8,128)(2,1)S(1)}, bf16[4,384,256]{2,1,0:T(8,128)(2,1)S(1)}, u32[]{:S(2)}, u32[]{:S(2)}) %collective-permute-start.10) | collective-permute-done | bytes 786464 | tf_op jit(solution)/shard_map/ppermute | solution.py:294
  80.1 5.4 %grads.3 = (bf16[3584,2048]{1,0:T(8,128)(2,1)}, bf16[3584,2048]{1,0:T(8,128)(2,1)}, f32[8,128]{1,0:T(8,128)S(1)}) custom-call(s32[2]{0:T(128)S(1)} %pad_add_fusion.where, bf16[256,2048]{1,0:T(8,128)(2,1)S(1)} %constant_dynamic-update-slice_fusion.tok, f32[28,1,2048]{2,1,0:T(1,128)S(1)} %bitcast.7, f32[28,1,2048]{2,1,0:T(1,128)S(1)} %bitcast.13, ...), custom_call_target="tpu_custom_call" | custom-call | flops 20000000000 | bytes 1 | tf_op jit(solution)/shard_map/grads/pallas_call | solution.py:263
  86.0 1.3 %collective-permute-start.11 = (bf16[4,256,256]{2,1,0:T(8,128)(2,1)S(1)}, bf16[4,256,256]{2,1,0:T(8,128)(2,1)S(1)}, u32[]{:S(2)}, u32[]{:S(2)}) collective-permute-start(bf16[4,256,256]{2,1,0:T(8,128)(2,1)S(1)} %sums.5.refs_1_), channel_id=1, source_target_pairs={{0,2},{2,0},{1,3},{3,1},{4,6},{6,4},{5,7},{7,5},{8,10},{10,8},{9,1... | collective-permute-start | bytes 1572872 | tf_op jit(solution)/shard_map/ppermute | solution.py:294
  87.2 1.4 %collective-permute-start.13 = (bf16[2,384,256]{2,1,0:T(8,128)(2,1)S(1)}, bf16[2,384,256]{2,1,0:T(8,128)(2,1)S(1)}, u32[]{:S(2)}, u32[]{:S(2)}) collective-permute-start(bf16[2,384,256]{2,1,0:T(8,128)(2,1)S(1)} %deltas.4.refs_4_.refs_0_), channel_id=1, source_target_pairs={{0,1},{1,0},{2,3},{3,2},{4,5},{5,4},{6,7},{7,6},{8,9},{9,8},{10,11... | collective-permute-start | bytes 1179656 | tf_op jit(solution)/shard_map/ppermute | solution.py:291
  89.7 3.2 %collective-permute-start.14 = (bf16[2,384,256]{2,1,0:T(8,128)(2,1)S(1)}, bf16[2,384,256]{2,1,0:T(8,128)(2,1)S(1)}, u32[]{:S(2)}, u32[]{:S(2)}) collective-permute-start(bf16[2,384,256]{2,1,0:T(8,128)(2,1)S(1)} %relay.4.refs_1_.refs_6_), channel_id=1, source_target_pairs={{0,1},{1,0},{2,3},{3,2},{4,5},{5,4},{6,7},{7,6},{8,9},{9,8},{10,11... | collective-permute-start | bytes 1179656 | tf_op jit(solution)/shard_map/ppermute | solution.py:291
  92.8 1.3 %collective-permute-done.14.refs_3_ = bf16[2,384,256]{2,1,0:T(8,128)(2,1)S(1)} collective-permute-done((bf16[2,384,256]{2,1,0:T(8,128)(2,1)S(1)}, bf16[2,384,256]{2,1,0:T(8,128)(2,1)S(1)}, u32[]{:S(2)}, u32[]{:S(2)}) %collective-permute-start.14) | collective-permute-done | bytes 393248 | tf_op jit(solution)/shard_map/ppermute | solution.py:291
  94.2 7.0 %grads.4 = (bf16[3584,2048]{1,0:T(8,128)(2,1)}, bf16[3584,2048]{1,0:T(8,128)(2,1)}, f32[8,128]{1,0:T(8,128)S(1)}) custom-call(s32[2]{0:T(128)S(1)} %pad_add_fusion.where, bf16[256,2048]{1,0:T(8,128)(2,1)S(1)} %constant_dynamic-update-slice_fusion.tok, f32[28,1,2048]{2,1,0:T(1,128)S(1)} %bitcast.8, ...), custom_call_target="tpu_custom_call", output_to_operand_aliasing={{0}: (8, {}), {1}: (9, {})} | custom-call | flops 1 | bytes 1 | tf_op jit(solution)/shard_map/grads/pallas_call | solution.py:263
  102.0 1.8 %collective-permute-start.16 = (bf16[2,256,256]{2,1,0:T(8,128)(2,1)S(1)}, bf16[2,256,256]{2,1,0:T(8,128)(2,1)S(1)}, u32[]{:S(2)}, u32[]{:S(2)}) collective-permute-start(bf16[2,256,256]{2,1,0:T(8,128)(2,1)S(1)} %deltas.5.refs_1_.refs_0_), channel_id=1, source_target_pairs={{0,1},{1,0},{2,3},{3,2},{4,5},{5,4},{6,7},{7,6},{8,9},{9,8},{10,11... | collective-permute-start | bytes 786440 | tf_op jit(solution)/shard_map/ppermute | solution.py:291
  103.8 4.4 %collective-permute-done.15.refs_0_ = bf16[2,256,256]{2,1,0:T(8,128)(2,1)S(1)} collective-permute-done((bf16[2,256,256]{2,1,0:T(8,128)(2,1)S(1)}, bf16[2,256,256]{2,1,0:T(8,128)(2,1)S(1)}, u32[]{:S(2)}, u32[]{:S(2)}) %collective-permute-start.15) | collective-permute-done | bytes 262176 | tf_op jit(solution)/shard_map/ppermute | solution.py:294
  108.2 2.4 %collective-permute-start.17 = (bf16[2,256,256]{2,1,0:T(8,128)(2,1)S(1)}, bf16[2,256,256]{2,1,0:T(8,128)(2,1)S(1)}, u32[]{:S(2)}, u32[]{:S(2)}) collective-permute-start(bf16[2,256,256]{2,1,0:T(8,128)(2,1)S(1)} %relay.5.refs_1_.refs_6_), channel_id=1, source_target_pairs={{0,1},{1,0},{2,3},{3,2},{4,5},{5,4},{6,7},{7,6},{8,9},{9,8},{10,11... | collective-permute-start | bytes 786440 | tf_op jit(solution)/shard_map/ppermute | solution.py:291
  110.7 1.2 collective-permute-done.17.refs_3_
  111.8 5.5 %grads.5 = (bf16[3584,2048]{1,0:T(8,128)(2,1)}, bf16[3584,2048]{1,0:T(8,128)(2,1)}, f32[8,128]{1,0:T(8,128)}) custom-call(s32[2]{0:T(128)S(1)} %pad_add_fusion.where, bf16[256,2048]{1,0:T(8,128)(2,1)S(1)} %constant_dynamic-update-slice_fusion.tok, f32[28,1,2048]{2,1,0:T(1,128)S(1)} %bitcast.9, ...), custom_call_target="tpu_custom_call", output_to_operand_aliasing={{0}: (8, {}), {1}: (9, {})} | custom-call | flops 1 | bytes 1 | tf_op jit(solution)/shard_map/grads/pallas_call | solution.py:263
  (38 shorter events, 9.0 us)
Async XLA Ops:
  0.6 13.1 %collective-permute-start.1 = (bf16[64,2048]{1,0:T(8,128)(2,1)}, bf16[64,2048]{1,0:T(8,128)(2,1)S(1)}, u32[]{:S(2)}, u32[]{:S(2)}) collective-permute-start(bf16[64,2048]{1,0:T(8,128)(2,1)} %param.7), channel_id=1, source_target_pairs={{0,8},{4,12},{8,0},{12,4},{1,9},{5,13},{9,1},{13,5},{2,10},{6,14},... | collective-permute-start | bytes 786440 | tf_op jit(solution)/shard_map/ppermute | solution.py:297
  0.8 12.9 %collective-permute-start = (bf16[64,2048]{1,0:T(8,128)(2,1)}, bf16[64,2048]{1,0:T(8,128)(2,1)S(1)}, u32[]{:S(2)}, u32[]{:S(2)}) collective-permute-start(bf16[64,2048]{1,0:T(8,128)(2,1)} %param.7), channel_id=1, source_target_pairs={{0,4},{4,0},{8,12},{12,8},{1,5},{5,1},{9,13},{13,9},{2,6},{6,2},{1... | collective-permute-start | bytes 786440 | tf_op jit(solution)/shard_map/ppermute | solution.py:297
  2.1 24.8 %collective-permute-start.2 = (bf16[64,2048]{1,0:T(8,128)(2,1)}, bf16[64,2048]{1,0:T(8,128)(2,1)S(1)}, u32[]{:S(2)}, u32[]{:S(2)}) collective-permute-start(bf16[64,2048]{1,0:T(8,128)(2,1)} %param.7), channel_id=1, source_target_pairs={{0,12},{4,8},{8,4},{12,0},{1,13},{5,9},{9,5},{13,1},{2,14},{6,10},... | collective-permute-start | bytes 786440 | tf_op jit(solution)/shard_map/ppermute | solution.py:297
  35.9 2.9 %collective-permute-start.3 = (bf16[2,4,256,256]{3,2,1,0:T(8,128)(2,1)S(1)}, bf16[2,4,256,256]{3,2,1,0:T(8,128)(2,1)S(1)}, u32[]{:S(2)}, u32[]{:S(2)}) collective-permute-start(bf16[2,4,256,256]{3,2,1,0:T(8,128)(2,1)S(1)} %get-tuple-element.17), channel_id=1, source_target_pairs={{0,1},{1,0},{2,3},{3,2},{4,5},{5,4},{6,7},{7,6},{8,9},{9,8},{10,11... | collective-permute-start | bytes 3145736 | tf_op jit(solution)/shard_map/ppermute | solution.py:291
  39.2 13.2 %collective-permute-start.5 = (bf16[4,256,256]{2,1,0:T(8,128)(2,1)S(1)}, bf16[4,256,256]{2,1,0:T(8,128)(2,1)S(1)}, u32[]{:S(2)}, u32[]{:S(2)}) collective-permute-start(bf16[4,256,256]{2,1,0:T(8,128)(2,1)S(1)} %sums.3.rest_0_), channel_id=1, source_target_pairs={{0,2},{2,0},{1,3},{3,1},{4,6},{6,4},{5,7},{7,5},{8,10},{10,8},{9,1... | collective-permute-start | bytes 1572872 | tf_op jit(solution)/shard_map/ppermute | solution.py:294
  51.5 3.8 %collective-permute-start.4 = (bf16[2,4,384,256]{3,2,1,0:T(8,128)(2,1)S(1)}, bf16[2,4,384,256]{3,2,1,0:T(8,128)(2,1)S(1)}, u32[]{:S(2)}, u32[]{:S(2)}) collective-permute-start(bf16[2,4,384,256]{3,2,1,0:T(8,128)(2,1)S(1)} %get-tuple-element.19), channel_id=1, source_target_pairs={{0,1},{1,0},{2,3},{3,2},{4,5},{5,4},{6,7},{7,6},{8,9},{9,8},{10,11... | collective-permute-start | bytes 4718600 | tf_op jit(solution)/shard_map/ppermute | solution.py:291
  52.9 27.2 %collective-permute-start.8 = (bf16[2,256,256]{2,1,0:T(8,128)(2,1)S(1)}, bf16[2,256,256]{2,1,0:T(8,128)(2,1)S(1)}, u32[]{:S(2)}, u32[]{:S(2)}) collective-permute-start(bf16[2,256,256]{2,1,0:T(8,128)(2,1)S(1)} %deltas.3.refs_2_.refs_0_), channel_id=1, source_target_pairs={{0,1},{1,0},{2,3},{3,2},{4,5},{5,4},{6,7},{7,6},{8,9},{9,8},{10,11... | collective-permute-start | bytes 786440 | tf_op jit(solution)/shard_map/ppermute | solution.py:291
  54.2 11.6 %collective-permute-start.7 = (bf16[2,256,256]{2,1,0:T(8,128)(2,1)S(1)}, bf16[2,256,256]{2,1,0:T(8,128)(2,1)S(1)}, u32[]{:S(2)}, u32[]{:S(2)}) collective-permute-start(bf16[2,256,256]{2,1,0:T(8,128)(2,1)S(1)} %deltas.3.refs_2_.refs_0_), channel_id=1, source_target_pairs={{0,2},{2,0},{1,3},{3,1},{4,6},{6,4},{5,7},{7,5},{8,10},{10,8},{9,1... | collective-permute-start | bytes 786440 | tf_op jit(solution)/shard_map/ppermute | solution.py:294
  55.8 23.2 %collective-permute-start.10 = (bf16[4,384,256]{2,1,0:T(8,128)(2,1)S(1)}, bf16[4,384,256]{2,1,0:T(8,128)(2,1)S(1)}, u32[]{:S(2)}, u32[]{:S(2)}) collective-permute-start(bf16[4,384,256]{2,1,0:T(8,128)(2,1)S(1)} %sums.4.rest_0_), channel_id=1, source_target_pairs={{0,2},{2,0},{1,3},{3,1},{4,6},{6,4},{5,7},{7,5},{8,10},{10,8},{9,1... | collective-permute-start | bytes 2359304 | tf_op jit(solution)/shard_map/ppermute | solution.py:294
  65.9 14.3 %collective-permute-start.9 = (bf16[2,256,256]{2,1,0:T(8,128)(2,1)S(1)}, bf16[2,256,256]{2,1,0:T(8,128)(2,1)S(1)}, u32[]{:S(2)}, u32[]{:S(2)}) collective-permute-start(bf16[2,256,256]{2,1,0:T(8,128)(2,1)S(1)} %relay.3.refs_1_), channel_id=1, source_target_pairs={{0,1},{1,0},{2,3},{3,2},{4,5},{5,4},{6,7},{7,6},{8,9},{9,8},{10,11... | collective-permute-start | bytes 786440 | tf_op jit(solution)/shard_map/ppermute | solution.py:291
  66.6 19.0 %collective-permute-start.6 = (bf16[2,4,256,256]{3,2,1,0:T(8,128)(2,1)S(1)}, bf16[2,4,256,256]{3,2,1,0:T(8,128)(2,1)S(1)}, u32[]{:S(2)}, u32[]{:S(2)}) collective-permute-start(bf16[2,4,256,256]{3,2,1,0:T(8,128)(2,1)S(1)} %get-tuple-element.21), channel_id=1, source_target_pairs={{0,1},{1,0},{2,3},{3,2},{4,5},{5,4},{6,7},{7,6},{8,9},{9,8},{10,11... | collective-permute-start | bytes 3145736 | tf_op jit(solution)/shard_map/ppermute | solution.py:291
  79.8 9.9 %collective-permute-start.12 = (bf16[2,384,256]{2,1,0:T(8,128)(2,1)S(1)}, bf16[2,384,256]{2,1,0:T(8,128)(2,1)S(1)}, u32[]{:S(2)}, u32[]{:S(2)}) collective-permute-start(bf16[2,384,256]{2,1,0:T(8,128)(2,1)S(1)} %deltas.4.refs_4_.refs_0_), channel_id=1, source_target_pairs={{0,2},{2,0},{1,3},{3,1},{4,6},{6,4},{5,7},{7,5},{8,10},{10,8},{9,1... | collective-permute-start | bytes 1179656 | tf_op jit(solution)/shard_map/ppermute | solution.py:294
  86.0 15.2 %collective-permute-start.11 = (bf16[4,256,256]{2,1,0:T(8,128)(2,1)S(1)}, bf16[4,256,256]{2,1,0:T(8,128)(2,1)S(1)}, u32[]{:S(2)}, u32[]{:S(2)}) collective-permute-start(bf16[4,256,256]{2,1,0:T(8,128)(2,1)S(1)} %sums.5.refs_1_), channel_id=1, source_target_pairs={{0,2},{2,0},{1,3},{3,1},{4,6},{6,4},{5,7},{7,5},{8,10},{10,8},{9,1... | collective-permute-start | bytes 1572872 | tf_op jit(solution)/shard_map/ppermute | solution.py:294
  87.2 5.6 %collective-permute-start.13 = (bf16[2,384,256]{2,1,0:T(8,128)(2,1)S(1)}, bf16[2,384,256]{2,1,0:T(8,128)(2,1)S(1)}, u32[]{:S(2)}, u32[]{:S(2)}) collective-permute-start(bf16[2,384,256]{2,1,0:T(8,128)(2,1)S(1)} %deltas.4.refs_4_.refs_0_), channel_id=1, source_target_pairs={{0,1},{1,0},{2,3},{3,2},{4,5},{5,4},{6,7},{7,6},{8,9},{9,8},{10,11... | collective-permute-start | bytes 1179656 | tf_op jit(solution)/shard_map/ppermute | solution.py:291
  89.7 4.5 %collective-permute-start.14 = (bf16[2,384,256]{2,1,0:T(8,128)(2,1)S(1)}, bf16[2,384,256]{2,1,0:T(8,128)(2,1)S(1)}, u32[]{:S(2)}, u32[]{:S(2)}) collective-permute-start(bf16[2,384,256]{2,1,0:T(8,128)(2,1)S(1)} %relay.4.refs_1_.refs_6_), channel_id=1, source_target_pairs={{0,1},{1,0},{2,3},{3,2},{4,5},{5,4},{6,7},{7,6},{8,9},{9,8},{10,11... | collective-permute-start | bytes 1179656 | tf_op jit(solution)/shard_map/ppermute | solution.py:291
  101.8 6.4 %collective-permute-start.15 = (bf16[2,256,256]{2,1,0:T(8,128)(2,1)S(1)}, bf16[2,256,256]{2,1,0:T(8,128)(2,1)S(1)}, u32[]{:S(2)}, u32[]{:S(2)}) collective-permute-start(bf16[2,256,256]{2,1,0:T(8,128)(2,1)S(1)} %deltas.5.refs_1_.refs_0_), channel_id=1, source_target_pairs={{0,2},{2,0},{1,3},{3,1},{4,6},{6,4},{5,7},{7,5},{8,10},{10,8},{9,1... | collective-permute-start | bytes 786440 | tf_op jit(solution)/shard_map/ppermute | solution.py:294
  102.0 8.7 %collective-permute-start.16 = (bf16[2,256,256]{2,1,0:T(8,128)(2,1)S(1)}, bf16[2,256,256]{2,1,0:T(8,128)(2,1)S(1)}, u32[]{:S(2)}, u32[]{:S(2)}) collective-permute-start(bf16[2,256,256]{2,1,0:T(8,128)(2,1)S(1)} %deltas.5.refs_1_.refs_0_), channel_id=1, source_target_pairs={{0,1},{1,0},{2,3},{3,2},{4,5},{5,4},{6,7},{7,6},{8,9},{9,8},{10,11... | collective-permute-start | bytes 786440 | tf_op jit(solution)/shard_map/ppermute | solution.py:291
  108.2 3.6 %collective-permute-start.17 = (bf16[2,256,256]{2,1,0:T(8,128)(2,1)S(1)}, bf16[2,256,256]{2,1,0:T(8,128)(2,1)S(1)}, u32[]{:S(2)}, u32[]{:S(2)}) collective-permute-start(bf16[2,256,256]{2,1,0:T(8,128)(2,1)S(1)} %relay.5.refs_1_.refs_6_), channel_id=1, source_target_pairs={{0,1},{1,0},{2,3},{3,2},{4,5},{5,4},{6,7},{7,6},{8,9},{9,8},{10,11... | collective-permute-start | bytes 786440 | tf_op jit(solution)/shard_map/ppermute | solution.py:291

commit v2 on v1

--- a/solution.py
+++ b/solution.py
@@ -12,7 +12,7 @@
 SLOTS = 6
 OUT_SLOTS = 4
 PARTS = (2, 3, 2)
-ORDER = ("F0", "S0", "F1+", "D0+", "S1", "F2+", "R0", "D1", "G0+", "S2", "R1", "G1", "D2", "R2", "G2")
+ORDER = ("F0", "S0", "F1+", "D0+", "S1", "F2+", "R0", "D1", "G0+", "S2", "R1", "G1", "D2", "H2", "R2", "K2")
 HBM = pl.BlockSpec(memory_space=pltpu.HBM)
 ANY = pl.BlockSpec(memory_space=pl.ANY)
 VM = pl.BlockSpec(memory_space=pltpu.VMEM)
@@ -189,7 +189,8 @@
     )(*pieces, *after)
 
 
-def grads_kernel(g, first, nx, nq, count, width, where, tok, mg, mu, *refs):
+def grads_kernel(g, first, nx, nq, places, width, where, tok, mg, mu, *refs):
+    count = len(places)
     deltas = refs[:count]
     gate, up, _, left, buf, in_sem, out_sem = refs[-7:]
     masks, outs = (mg, mu), (gate, up)
@@ -200,9 +201,9 @@
         copy.start()
 
     groups = []
-    for b in range(count):
-        side = lax.rem(where[0] + b // nx, 2)
-        groups.append(first + (side * nx + lax.rem(where[1] + nx - b % nx, nx)) * nq)
+    for other, k in places:
+        side = lax.rem(where[0] + other, 2)
+        groups.append(first + (side * nx + lax.rem(where[1] + nx - k, nx)) * nq)
 
     def columns(t):
         return pl.ds(pl.multiple_of((t // 2) * width, width), width)
@@ -252,7 +253,7 @@
             copy.wait()
 
 
-def grads_call(g, first, nx, nq, where, tok, masks, deltas, grads, shape, after, cost):
+def grads_call(g, first, nx, nq, where, tok, masks, deltas, places, grads, shape, after, cost):
     tokens, depth = tok.shape
     rows = nq * g
     count = len(deltas)
@@ -261,7 +262,7 @@
     base = 4 + count
     grad = jax.ShapeDtypeStruct(shape, jnp.bfloat16)
     return pl.pallas_call(
-        functools.partial(grads_kernel, g, first, nx, nq, count, width),
+        functools.partial(grads_kernel, g, first, nx, nq, places, width),
         in_specs=[SM, VM, VM, VM] + [ANY] * count + [HBM] * len(held) + [ANY] * len(after),
         out_specs=(HBM, HBM, ANY),
         out_shape=(grad, grad, jax.ShapeDtypeStruct((8, BLOCK), jnp.float32)),
@@ -333,8 +334,14 @@
             state[u] = [mine, *near, theirs, *[swap(x) for x in near]]
             after = (near[0],)
         else:
+            near = [k for k in range(nx) if kind == "G" or (k == 0) == (kind == "H")]
+            places = tuple((other, k) for other in range(2) for k in near)
+            if kind == "H":
+                pieces = state[u][0]
+            else:
+                pieces = [state[u][other * nx + k] for other, k in places]
             *grads, done = grads_call(
-                g, first, nx, nq, where, tok, masks, state[u], grads, (local_ff, local_d), after, cost
+                g, first, nx, nq, where, tok, masks, pieces, places, grads, (local_ff, local_d), after, cost
             )
             after = (done,)
     return tuple(grads)

time: 118 us -> 118 us (level)
  Pallas kernels: 50.8 us -> 53.2 us
  starting transfers between devices: 18.5 us -> 16.8 us
    pallas_call x3 -> x4, Pallas kernels: 17.9 us -> 20.3 us  [grads_call(): pl.pallas_call(functools.partial(grads_kernel, g, first, nx, nq, places,...]
    ppermute x9, starting transfers between devices: 12.1 us -> 10.3 us  [swap(): return lax.ppermute(x, 'sub', [(0, 1), (1, 0)])]
    ppermute x6, waiting for transfers between devices: 17.9 us -> 16.2 us  [turn(): return lax.ppermute(x, 'col', [(i, (i + k) % nx) for i in range(nx)])]
  transfers between devices with their start and end apart: 18 -> 18, of which waited for: 10 -> 11; matrix products, arithmetic and copies ran while one was open for 3% -> 3% of each run, Pallas kernels for 30% -> 34%
where the time goes in v2:
time: 118 us; the launch traced here: 117 us
  Pallas kernels  53.2 us (45%)
  waiting for transfers between devices  43.2 us (37%)
  starting transfers between devices  16.8 us (14%)
  other arithmetic  1.92 us (2%)
  local copies, waits for them, and re-layouts  1.29 us (1%)
    pallas_call x3, Pallas kernels, forward_call(): pl.pallas_call(functools.partial(forward_kernel, g, first, nx, nq), in_sp...  29.5 us
    ppermute x3, waiting for transfers between devices, per_device(): lax.ppermute(tokens, 'grid', [(i, i ^ k) for i in range(nz)])  20.5 us
    pallas_call x4, Pallas kernels, grads_call(): pl.pallas_call(functools.partial(grads_kernel, g, first, nx, nq, places,...  20.3 us
    ppermute x6, waiting for transfers between devices, turn(): return lax.ppermute(x, 'col', [(i, (i + k) % nx) for i in range(nx)])  16.2 us
    ppermute x9, starting transfers between devices, swap(): return lax.ppermute(x, 'sub', [(0, 1), (1, 0)])  10.3 us
    ppermute x9, waiting for transfers between devices, swap(): return lax.ppermute(x, 'sub', [(0, 1), (1, 0)])  6.42 us
    ppermute x6, starting transfers between devices, turn(): return lax.ppermute(x, 'col', [(i, (i + k) % nx) for i in range(nx)])  3.73 us
    ppermute x3, starting transfers between devices, per_device(): lax.ppermute(tokens, 'grid', [(i, i ^ k) for i in range(nz)])  2.71 us
  transfers between devices with their start and end apart: 18, of which 11 were waited for; matrix products, arithmetic and copies ran while one was open for 3% of the time, Pallas kernels for 34%

profile of v2, /device:TPU:19, one launch (start us, length us, event | category | flops | bytes accessed | tf_op | source)
XLA Modules:
  0.0 117.2 jit_solution(8345794232838478289)
XLA Ops:
  0.8 1.3 %collective-permute-start = (bf16[64,2048]{1,0:T(8,128)(2,1)}, bf16[64,2048]{1,0:T(8,128)(2,1)S(1)}, u32[]{:S(2)}, u32[]{:S(2)}) collective-permute-start(bf16[64,2048]{1,0:T(8,128)(2,1)} %param.7), channel_id=1, source_target_pairs={{0,4},{4,0},{8,12},{12,8},{1,5},{5,1},{9,13},{13,9},{2,6},{6,2},{1... | collective-permute-start | bytes 786440 | tf_op jit(solution)/shard_map/ppermute | solution.py:298
  2.1 1.3 %collective-permute-start.2 = (bf16[64,2048]{1,0:T(8,128)(2,1)}, bf16[64,2048]{1,0:T(8,128)(2,1)S(1)}, u32[]{:S(2)}, u32[]{:S(2)}) collective-permute-start(bf16[64,2048]{1,0:T(8,128)(2,1)} %param.7), channel_id=1, source_target_pairs={{0,12},{4,8},{8,4},{12,0},{1,13},{5,9},{9,5},{13,1},{2,14},{6,10},... | collective-permute-start | bytes 786440 | tf_op jit(solution)/shard_map/ppermute | solution.py:298
  3.3 1.0 constant_dynamic-update-slice_fusion.3
  4.4 1.8 %compare_reduce_fusion = (pred[28,16]{1,0:T(8,128)(4,1)S(1)}, pred[28,16]{1,0:T(8,128)(4,1)S(1)}) fusion(s32[28,64]{1,0:T(8,128)} %param.13, s32[16]{0:T(128)S(1)} %iota_add_fusion, s32[28,64]{1,0:T(8,128)} %param.12), kind=kLoop, calls=%fused_computation | loop fusion | flops 113792 | bytes 15296 | tf_op jit(solution)/shard_map/reduce_or | solution.py:30
  6.3 7.4 %collective-permute-done = bf16[64,2048]{1,0:T(8,128)(2,1)S(1)} collective-permute-done((bf16[64,2048]{1,0:T(8,128)(2,1)}, bf16[64,2048]{1,0:T(8,128)(2,1)S(1)}, u32[]{:S(2)}, u32[]{:S(2)}) %collective-permute-start) | collective-permute-done | bytes 262176 | tf_op jit(solution)/shard_map/ppermute | solution.py:298
  13.7 13.2 %collective-permute-done.2 = bf16[64,2048]{1,0:T(8,128)(2,1)S(1)} collective-permute-done((bf16[64,2048]{1,0:T(8,128)(2,1)}, bf16[64,2048]{1,0:T(8,128)(2,1)S(1)}, u32[]{:S(2)}, u32[]{:S(2)}) %collective-permute-start.2) | collective-permute-done | bytes 262176 | tf_op jit(solution)/shard_map/ppermute | solution.py:298
  27.2 8.8 %forward.3 = (bf16[2,4,256,256]{3,2,1,0:T(8,128)(2,1)S(1)}, bf16[2,4,256,256]{3,2,1,0:T(8,128)(2,1)S(1)}) custom-call(s32[2]{0:T(128)S(1)} %pad_add_fusion.where, bf16[256,2048]{1,0:T(8,128)(2,1)S(1)} %constant_dynamic-update-slice_fusion.tok, f32[28,1,2048]{2,1,0:T(1,128)S(1)} %bitcast.4, f32[28,1,2048]{2,1,0:T(1,128)S(1)} %bitcast.11, ...), custom_call_target="tpu_custom_call" | custom-call | flops 1 | bytes 1 | tf_op jit(solution)/shard_map/forward/pallas_call | solution.py:98
  36.5 2.3 %collective-permute-done.3.refs_1_.got = bf16[2,4,256,256]{3,2,1,0:T(8,128)(2,1)S(1)} collective-permute-done((bf16[2,4,256,256]{3,2,1,0:T(8,128)(2,1)S(1)}, bf16[2,4,256,256]{3,2,1,0:T(8,128)(2,1)S(1)}, u32[]{:S(2)}, u32[]{:S(2)}) %collective-permute-start.3) | collective-permute-done | bytes 1048608 | tf_op jit(solution)/shard_map/ppermute | solution.py:292
  39.5 12.0 %forward.4 = (bf16[2,4,384,256]{3,2,1,0:T(8,128)(2,1)S(1)}, bf16[2,4,384,256]{3,2,1,0:T(8,128)(2,1)S(1)}) custom-call(s32[2]{0:T(128)S(1)} %pad_add_fusion.where, bf16[256,2048]{1,0:T(8,128)(2,1)S(1)} %constant_dynamic-update-slice_fusion.tok, f32[28,1,2048]{2,1,0:T(1,128)S(1)} %bitcast.5, f32[28,1,2048]{2,1,0:T(1,128)S(1)} %bitcast.12, ...), custom_call_target="tpu_custom_call" | custom-call | flops 20000000000 | bytes 1 | tf_op jit(solution)/shard_map/forward/pallas_call | solution.py:98
  52.9 1.3 %collective-permute-start.8 = (bf16[2,256,256]{2,1,0:T(8,128)(2,1)S(1)}, bf16[2,256,256]{2,1,0:T(8,128)(2,1)S(1)}, u32[]{:S(2)}, u32[]{:S(2)}) collective-permute-start(bf16[2,256,256]{2,1,0:T(8,128)(2,1)S(1)} %deltas.3.refs_2_.refs_0_), channel_id=1, source_target_pairs={{0,1},{1,0},{2,3},{3,2},{4,5},{5,4},{6,7},{7,6},{8,9},{9,8},{10,11... | collective-permute-start | bytes 786440 | tf_op jit(solution)/shard_map/ppermute | solution.py:292
  55.8 1.3 %collective-permute-start.10 = (bf16[4,384,256]{2,1,0:T(8,128)(2,1)S(1)}, bf16[4,384,256]{2,1,0:T(8,128)(2,1)S(1)}, u32[]{:S(2)}, u32[]{:S(2)}) collective-permute-start(bf16[4,384,256]{2,1,0:T(8,128)(2,1)S(1)} %sums.4.rest_0_), channel_id=1, source_target_pairs={{0,2},{2,0},{1,3},{3,1},{4,6},{6,4},{5,7},{7,5},{8,10},{10,8},{9,1... | collective-permute-start | bytes 2359304 | tf_op jit(solution)/shard_map/ppermute | solution.py:295
  57.1 8.8 %forward.5 = (bf16[2,4,256,256]{3,2,1,0:T(8,128)(2,1)S(1)}, bf16[2,4,256,256]{3,2,1,0:T(8,128)(2,1)S(1)}) custom-call(s32[2]{0:T(128)S(1)} %pad_add_fusion.where, bf16[256,2048]{1,0:T(8,128)(2,1)S(1)} %constant_dynamic-update-slice_fusion.tok, f32[28,1,2048]{2,1,0:T(1,128)S(1)} %bitcast.6, f32[28,1,2048]{2,1,0:T(1,128)S(1)} %bitcast.13, ...), custom_call_target="tpu_custom_call" | custom-call | flops 20000000000 | bytes 1 | tf_op jit(solution)/shard_map/forward/pallas_call | solution.py:98
  66.7 12.3 %collective-permute-done.10.refs_0_ = bf16[4,384,256]{2,1,0:T(8,128)(2,1)S(1)} collective-permute-done((bf16[4,384,256]{2,1,0:T(8,128)(2,1)S(1)}, bf16[4,384,256]{2,1,0:T(8,128)(2,1)S(1)}, u32[]{:S(2)}, u32[]{:S(2)}) %collective-permute-start.10) | collective-permute-done | bytes 786464 | tf_op jit(solution)/shard_map/ppermute | solution.py:295
  80.1 5.4 %grads.4 = (bf16[3584,2048]{1,0:T(8,128)(2,1)}, bf16[3584,2048]{1,0:T(8,128)(2,1)}, f32[8,128]{1,0:T(8,128)S(1)}) custom-call(s32[2]{0:T(128)S(1)} %pad_add_fusion.where, bf16[256,2048]{1,0:T(8,128)(2,1)S(1)} %constant_dynamic-update-slice_fusion.tok, f32[28,1,2048]{2,1,0:T(1,128)S(1)} %bitcast.7, f32[28,1,2048]{2,1,0:T(1,128)S(1)} %bitcast.14, ...), custom_call_target="tpu_custom_call" | custom-call | flops 20000000000 | bytes 1 | tf_op jit(solution)/shard_map/grads/pallas_call | solution.py:264
  86.0 1.3 %collective-permute-start.11 = (bf16[4,256,256]{2,1,0:T(8,128)(2,1)S(1)}, bf16[4,256,256]{2,1,0:T(8,128)(2,1)S(1)}, u32[]{:S(2)}, u32[]{:S(2)}) collective-permute-start(bf16[4,256,256]{2,1,0:T(8,128)(2,1)S(1)} %sums.5.refs_1_), channel_id=1, source_target_pairs={{0,2},{2,0},{1,3},{3,1},{4,6},{6,4},{5,7},{7,5},{8,10},{10,8},{9,1... | collective-permute-start | bytes 1572872 | tf_op jit(solution)/shard_map/ppermute | solution.py:295
  87.2 1.4 %collective-permute-start.13 = (bf16[2,384,256]{2,1,0:T(8,128)(2,1)S(1)}, bf16[2,384,256]{2,1,0:T(8,128)(2,1)S(1)}, u32[]{:S(2)}, u32[]{:S(2)}) collective-permute-start(bf16[2,384,256]{2,1,0:T(8,128)(2,1)S(1)} %deltas.4.refs_4_.refs_0_), channel_id=1, source_target_pairs={{0,1},{1,0},{2,3},{3,2},{4,5},{5,4},{6,7},{7,6},{8,9},{9,8},{10,11... | collective-permute-start | bytes 1179656 | tf_op jit(solution)/shard_map/ppermute | solution.py:292
  89.7 3.2 %collective-permute-start.14 = (bf16[2,384,256]{2,1,0:T(8,128)(2,1)S(1)}, bf16[2,384,256]{2,1,0:T(8,128)(2,1)S(1)}, u32[]{:S(2)}, u32[]{:S(2)}) collective-permute-start(bf16[2,384,256]{2,1,0:T(8,128)(2,1)S(1)} %relay.4.refs_1_.refs_6_), channel_id=1, source_target_pairs={{0,1},{1,0},{2,3},{3,2},{4,5},{5,4},{6,7},{7,6},{8,9},{9,8},{10,11... | collective-permute-start | bytes 1179656 | tf_op jit(solution)/shard_map/ppermute | solution.py:292
  92.8 1.3 %collective-permute-done.14.refs_3_ = bf16[2,384,256]{2,1,0:T(8,128)(2,1)S(1)} collective-permute-done((bf16[2,384,256]{2,1,0:T(8,128)(2,1)S(1)}, bf16[2,384,256]{2,1,0:T(8,128)(2,1)S(1)}, u32[]{:S(2)}, u32[]{:S(2)}) %collective-permute-start.14) | collective-permute-done | bytes 393248 | tf_op jit(solution)/shard_map/ppermute | solution.py:292
  94.2 7.0 %grads.5 = (bf16[3584,2048]{1,0:T(8,128)(2,1)}, bf16[3584,2048]{1,0:T(8,128)(2,1)}, f32[8,128]{1,0:T(8,128)S(1)}) custom-call(s32[2]{0:T(128)S(1)} %pad_add_fusion.where, bf16[256,2048]{1,0:T(8,128)(2,1)S(1)} %constant_dynamic-update-slice_fusion.tok, f32[28,1,2048]{2,1,0:T(1,128)S(1)} %bitcast.8, ...), custom_call_target="tpu_custom_call", output_to_operand_aliasing={{0}: (8, {}), {1}: (9, {})} | custom-call | flops 1 | bytes 1 | tf_op jit(solution)/shard_map/grads/pallas_call | solution.py:264
  101.8 1.5 %collective-permute-start.16 = (bf16[2,256,256]{2,1,0:T(8,128)(2,1)S(1)}, bf16[2,256,256]{2,1,0:T(8,128)(2,1)S(1)}, u32[]{:S(2)}, u32[]{:S(2)}) collective-permute-start(bf16[2,256,256]{2,1,0:T(8,128)(2,1)S(1)} %deltas.5.refs_0_.refs_4_), channel_id=1, source_target_pairs={{0,1},{1,0},{2,3},{3,2},{4,5},{5,4},{6,7},{7,6},{8,9},{9,8},{10,11... | collective-permute-start | bytes 786440 | tf_op jit(solution)/shard_map/ppermute | solution.py:292
  104.4 4.0 %grads.6 = (bf16[3584,2048]{1,0:T(8,128)(2,1)}, bf16[3584,2048]{1,0:T(8,128)(2,1)}, f32[8,128]{1,0:T(8,128)S(1)}) custom-call(s32[2]{0:T(128)S(1)} %pad_add_fusion.where, bf16[256,2048]{1,0:T(8,128)(2,1)S(1)} %constant_dynamic-update-slice_fusion.tok, f32[28,1,2048]{2,1,0:T(1,128)S(1)} %bitcast.9, ...), custom_call_target="tpu_custom_call", output_to_operand_aliasing={{0}: (6, {}), {1}: (7, {})} | custom-call | flops 1 | bytes 1 | tf_op jit(solution)/shard_map/grads/pallas_call | solution.py:264
  108.4 2.7 %collective-permute-done.15.refs_0_ = bf16[2,256,256]{2,1,0:T(8,128)(2,1)S(1)} collective-permute-done((bf16[2,256,256]{2,1,0:T(8,128)(2,1)S(1)}, bf16[2,256,256]{2,1,0:T(8,128)(2,1)S(1)}, u32[]{:S(2)}, u32[]{:S(2)}) %collective-permute-start.15) | collective-permute-done | bytes 262176 | tf_op jit(solution)/shard_map/ppermute | solution.py:295
  112.1 1.2 collective-permute-done.17.refs_1_
  113.3 4.0 %grads.7 = (bf16[3584,2048]{1,0:T(8,128)(2,1)}, bf16[3584,2048]{1,0:T(8,128)(2,1)}, f32[8,128]{1,0:T(8,128)}) custom-call(s32[2]{0:T(128)S(1)} %pad_add_fusion.where, bf16[256,2048]{1,0:T(8,128)(2,1)S(1)} %constant_dynamic-update-slice_fusion.tok, f32[28,1,2048]{2,1,0:T(1,128)S(1)} %bitcast.10, ...), custom_call_target="tpu_custom_call", output_to_operand_aliasing={{0}: (6, {}), {1}: (7, {})} | custom-call | flops 1 | bytes 1 | tf_op jit(solution)/shard_map/grads/pallas_call | solution.py:264
  (39 shorter events, 10.9 us)
Async XLA Ops:
  0.6 13.1 %collective-permute-start.1 = (bf16[64,2048]{1,0:T(8,128)(2,1)}, bf16[64,2048]{1,0:T(8,128)(2,1)S(1)}, u32[]{:S(2)}, u32[]{:S(2)}) collective-permute-start(bf16[64,2048]{1,0:T(8,128)(2,1)} %param.7), channel_id=1, source_target_pairs={{0,8},{4,12},{8,0},{12,4},{1,9},{5,13},{9,1},{13,5},{2,10},{6,14},... | collective-permute-start | bytes 786440 | tf_op jit(solution)/shard_map/ppermute | solution.py:298
  0.8 12.9 %collective-permute-start = (bf16[64,2048]{1,0:T(8,128)(2,1)}, bf16[64,2048]{1,0:T(8,128)(2,1)S(1)}, u32[]{:S(2)}, u32[]{:S(2)}) collective-permute-start(bf16[64,2048]{1,0:T(8,128)(2,1)} %param.7), channel_id=1, source_target_pairs={{0,4},{4,0},{8,12},{12,8},{1,5},{5,1},{9,13},{13,9},{2,6},{6,2},{1... | collective-permute-start | bytes 786440 | tf_op jit(solution)/shard_map/ppermute | solution.py:298
  2.1 24.8 %collective-permute-start.2 = (bf16[64,2048]{1,0:T(8,128)(2,1)}, bf16[64,2048]{1,0:T(8,128)(2,1)S(1)}, u32[]{:S(2)}, u32[]{:S(2)}) collective-permute-start(bf16[64,2048]{1,0:T(8,128)(2,1)} %param.7), channel_id=1, source_target_pairs={{0,12},{4,8},{8,4},{12,0},{1,13},{5,9},{9,5},{13,1},{2,14},{6,10},... | collective-permute-start | bytes 786440 | tf_op jit(solution)/shard_map/ppermute | solution.py:298
  35.9 2.9 %collective-permute-start.3 = (bf16[2,4,256,256]{3,2,1,0:T(8,128)(2,1)S(1)}, bf16[2,4,256,256]{3,2,1,0:T(8,128)(2,1)S(1)}, u32[]{:S(2)}, u32[]{:S(2)}) collective-permute-start(bf16[2,4,256,256]{3,2,1,0:T(8,128)(2,1)S(1)} %get-tuple-element.20), channel_id=1, source_target_pairs={{0,1},{1,0},{2,3},{3,2},{4,5},{5,4},{6,7},{7,6},{8,9},{9,8},{10,11... | collective-permute-start | bytes 3145736 | tf_op jit(solution)/shard_map/ppermute | solution.py:292
  39.2 13.2 %collective-permute-start.5 = (bf16[4,256,256]{2,1,0:T(8,128)(2,1)S(1)}, bf16[4,256,256]{2,1,0:T(8,128)(2,1)S(1)}, u32[]{:S(2)}, u32[]{:S(2)}) collective-permute-start(bf16[4,256,256]{2,1,0:T(8,128)(2,1)S(1)} %sums.3.rest_0_), channel_id=1, source_target_pairs={{0,2},{2,0},{1,3},{3,1},{4,6},{6,4},{5,7},{7,5},{8,10},{10,8},{9,1... | collective-permute-start | bytes 1572872 | tf_op jit(solution)/shard_map/ppermute | solution.py:295
  51.5 3.8 %collective-permute-start.4 = (bf16[2,4,384,256]{3,2,1,0:T(8,128)(2,1)S(1)}, bf16[2,4,384,256]{3,2,1,0:T(8,128)(2,1)S(1)}, u32[]{:S(2)}, u32[]{:S(2)}) collective-permute-start(bf16[2,4,384,256]{3,2,1,0:T(8,128)(2,1)S(1)} %get-tuple-element.22), channel_id=1, source_target_pairs={{0,1},{1,0},{2,3},{3,2},{4,5},{5,4},{6,7},{7,6},{8,9},{9,8},{10,11... | collective-permute-start | bytes 4718600 | tf_op jit(solution)/shard_map/ppermute | solution.py:292
  52.9 27.2 %collective-permute-start.8 = (bf16[2,256,256]{2,1,0:T(8,128)(2,1)S(1)}, bf16[2,256,256]{2,1,0:T(8,128)(2,1)S(1)}, u32[]{:S(2)}, u32[]{:S(2)}) collective-permute-start(bf16[2,256,256]{2,1,0:T(8,128)(2,1)S(1)} %deltas.3.refs_2_.refs_0_), channel_id=1, source_target_pairs={{0,1},{1,0},{2,3},{3,2},{4,5},{5,4},{6,7},{7,6},{8,9},{9,8},{10,11... | collective-permute-start | bytes 786440 | tf_op jit(solution)/shard_map/ppermute | solution.py:292
  54.2 11.6 %collective-permute-start.7 = (bf16[2,256,256]{2,1,0:T(8,128)(2,1)S(1)}, bf16[2,256,256]{2,1,0:T(8,128)(2,1)S(1)}, u32[]{:S(2)}, u32[]{:S(2)}) collective-permute-start(bf16[2,256,256]{2,1,0:T(8,128)(2,1)S(1)} %deltas.3.refs_2_.refs_0_), channel_id=1, source_target_pairs={{0,2},{2,0},{1,3},{3,1},{4,6},{6,4},{5,7},{7,5},{8,10},{10,8},{9,1... | collective-permute-start | bytes 786440 | tf_op jit(solution)/shard_map/ppermute | solution.py:295
  55.8 23.2 %collective-permute-start.10 = (bf16[4,384,256]{2,1,0:T(8,128)(2,1)S(1)}, bf16[4,384,256]{2,1,0:T(8,128)(2,1)S(1)}, u32[]{:S(2)}, u32[]{:S(2)}) collective-permute-start(bf16[4,384,256]{2,1,0:T(8,128)(2,1)S(1)} %sums.4.rest_0_), channel_id=1, source_target_pairs={{0,2},{2,0},{1,3},{3,1},{4,6},{6,4},{5,7},{7,5},{8,10},{10,8},{9,1... | collective-permute-start | bytes 2359304 | tf_op jit(solution)/shard_map/ppermute | solution.py:295
  65.9 14.3 %collective-permute-start.9 = (bf16[2,256,256]{2,1,0:T(8,128)(2,1)S(1)}, bf16[2,256,256]{2,1,0:T(8,128)(2,1)S(1)}, u32[]{:S(2)}, u32[]{:S(2)}) collective-permute-start(bf16[2,256,256]{2,1,0:T(8,128)(2,1)S(1)} %relay.3.refs_1_), channel_id=1, source_target_pairs={{0,1},{1,0},{2,3},{3,2},{4,5},{5,4},{6,7},{7,6},{8,9},{9,8},{10,11... | collective-permute-start | bytes 786440 | tf_op jit(solution)/shard_map/ppermute | solution.py:292
  66.6 19.0 %collective-permute-start.6 = (bf16[2,4,256,256]{3,2,1,0:T(8,128)(2,1)S(1)}, bf16[2,4,256,256]{3,2,1,0:T(8,128)(2,1)S(1)}, u32[]{:S(2)}, u32[]{:S(2)}) collective-permute-start(bf16[2,4,256,256]{3,2,1,0:T(8,128)(2,1)S(1)} %get-tuple-element.24), channel_id=1, source_target_pairs={{0,1},{1,0},{2,3},{3,2},{4,5},{5,4},{6,7},{7,6},{8,9},{9,8},{10,11... | collective-permute-start | bytes 3145736 | tf_op jit(solution)/shard_map/ppermute | solution.py:292
  79.8 9.9 %collective-permute-start.12 = (bf16[2,384,256]{2,1,0:T(8,128)(2,1)S(1)}, bf16[2,384,256]{2,1,0:T(8,128)(2,1)S(1)}, u32[]{:S(2)}, u32[]{:S(2)}) collective-permute-start(bf16[2,384,256]{2,1,0:T(8,128)(2,1)S(1)} %deltas.4.refs_4_.refs_0_), channel_id=1, source_target_pairs={{0,2},{2,0},{1,3},{3,1},{4,6},{6,4},{5,7},{7,5},{8,10},{10,8},{9,1... | collective-permute-start | bytes 1179656 | tf_op jit(solution)/shard_map/ppermute | solution.py:295
  86.0 15.2 %collective-permute-start.11 = (bf16[4,256,256]{2,1,0:T(8,128)(2,1)S(1)}, bf16[4,256,256]{2,1,0:T(8,128)(2,1)S(1)}, u32[]{:S(2)}, u32[]{:S(2)}) collective-permute-start(bf16[4,256,256]{2,1,0:T(8,128)(2,1)S(1)} %sums.5.refs_1_), channel_id=1, source_target_pairs={{0,2},{2,0},{1,3},{3,1},{4,6},{6,4},{5,7},{7,5},{8,10},{10,8},{9,1... | collective-permute-start | bytes 1572872 | tf_op jit(solution)/shard_map/ppermute | solution.py:295
  87.2 5.6 %collective-permute-start.13 = (bf16[2,384,256]{2,1,0:T(8,128)(2,1)S(1)}, bf16[2,384,256]{2,1,0:T(8,128)(2,1)S(1)}, u32[]{:S(2)}, u32[]{:S(2)}) collective-permute-start(bf16[2,384,256]{2,1,0:T(8,128)(2,1)S(1)} %deltas.4.refs_4_.refs_0_), channel_id=1, source_target_pairs={{0,1},{1,0},{2,3},{3,2},{4,5},{5,4},{6,7},{7,6},{8,9},{9,8},{10,11... | collective-permute-start | bytes 1179656 | tf_op jit(solution)/shard_map/ppermute | solution.py:292
  89.7 4.5 %collective-permute-start.14 = (bf16[2,384,256]{2,1,0:T(8,128)(2,1)S(1)}, bf16[2,384,256]{2,1,0:T(8,128)(2,1)S(1)}, u32[]{:S(2)}, u32[]{:S(2)}) collective-permute-start(bf16[2,384,256]{2,1,0:T(8,128)(2,1)S(1)} %relay.4.refs_1_.refs_6_), channel_id=1, source_target_pairs={{0,1},{1,0},{2,3},{3,2},{4,5},{5,4},{6,7},{7,6},{8,9},{9,8},{10,11... | collective-permute-start | bytes 1179656 | tf_op jit(solution)/shard_map/ppermute | solution.py:292
  101.8 2.7 %collective-permute-start.16 = (bf16[2,256,256]{2,1,0:T(8,128)(2,1)S(1)}, bf16[2,256,256]{2,1,0:T(8,128)(2,1)S(1)}, u32[]{:S(2)}, u32[]{:S(2)}) collective-permute-start(bf16[2,256,256]{2,1,0:T(8,128)(2,1)S(1)} %deltas.5.refs_0_.refs_4_), channel_id=1, source_target_pairs={{0,1},{1,0},{2,3},{3,2},{4,5},{5,4},{6,7},{7,6},{8,9},{9,8},{10,11... | collective-permute-start | bytes 786440 | tf_op jit(solution)/shard_map/ppermute | solution.py:292
  103.3 7.9 %collective-permute-start.15 = (bf16[2,256,256]{2,1,0:T(8,128)(2,1)S(1)}, bf16[2,256,256]{2,1,0:T(8,128)(2,1)S(1)}, u32[]{:S(2)}, u32[]{:S(2)}) collective-permute-start(bf16[2,256,256]{2,1,0:T(8,128)(2,1)S(1)} %deltas.5.refs_0_.refs_4_), channel_id=1, source_target_pairs={{0,2},{2,0},{1,3},{3,1},{4,6},{6,4},{5,7},{7,5},{8,10},{10,8},{9,1... | collective-permute-start | bytes 786440 | tf_op jit(solution)/shard_map/ppermute | solution.py:295
  111.2 2.1 %collective-permute-start.17 = (bf16[2,256,256]{2,1,0:T(8,128)(2,1)S(1)}, bf16[2,256,256]{2,1,0:T(8,128)(2,1)S(1)}, u32[]{:S(2)}, u32[]{:S(2)}) collective-permute-start(bf16[2,256,256]{2,1,0:T(8,128)(2,1)S(1)} %relay.5.refs_0_.refs_4_), channel_id=1, source_target_pairs={{0,1},{1,0},{2,3},{3,2},{4,5},{5,4},{6,7},{7,6},{8,9},{9,8},{10,11... | collective-permute-start | bytes 786440 | tf_op jit(solution)/shard_map/ppermute | solution.py:292
